TPU v7x, 128 devices: a whole 4x4x4 slice. The times are simulated.
128 devices in a mesh: item: 32 (over z, x, core), req: 4 (over y).
Axes of the slice: x: 4, y: 4, z: 4, core: 2. Of those that a mesh axis runs over, the one named last changes fastest.
Arguments:
- user_emb: bfloat16 [128, 256], P('req'), may hold values from -6 to 6
- codebooks: bfloat16 [32, 256, 8], P('item'), may hold values from -1 to 1
- item_codes: int32 [131072, 32], P('item'), may hold values from 0 to 255
- item_place: int32 [131072], replicated, may hold values from 0 to 131071, as said below
- candidates: int32 [128, 512], P('req', 'item'), may hold values from 0 to 131071, as said below
- item_features: bfloat16 [131072, 768], P(('item', 'req')), may hold values from -6 to 6
- cross_weights: bfloat16 [4, 1024, 1024], replicated, may hold values from -0.25 to 0.25
- cross_bias: float32 [4, 1024], replicated, may hold values from -6 to 6
- out_weight: float32 [1024], replicated, may hold values from -0.5 to 0.5
Outputs:
- scores: float32 [128, 131072], P('req', 'item')
- logits: float32 [128, 512], P('req', 'item')
Inputs may be any that keep to these rules, and one draw needn't show every extreme that they name: A permutation of the item ids: item_place[i] is the storage row of item i; storage row s is held by the device at flat index s // 1024 of item+req (item slowest). Item ids. In each aligned block of 32 requests by 16 candidates (one device's share), at most 12 candidates have storage rows on any one owner; in every draw one owner, the same for all blocks, is named exactly 12 times in every block.
All inputs are finite; a program needn't handle non-finite values.
Results may differ from a plain program's by a relative error of at most 0.0033.
Values may be sent and summed in bfloat16 or wider, within the bound.
No kernel may reach another device: no remote copies, remote signals or barrier semaphores. Data moves between devices by JAX's collectives and lax.ppermute only.
A program may use at most 64 MiB of HBM per device.

v0:
```python
import jax
import jax.numpy as jnp
from jax import lax
from jax.sharding import PartitionSpec as P

M = 32


def score_tables(total, tables, item_codes):
    width_all = tables.shape[1]
    codes_count = tables.shape[2]
    code_range = lax.iota(jnp.int32, codes_count)[None, None, :]
    for group in range(0, width_all, 4):
        width = min(4, width_all - group)
        codes_now = lax.dynamic_slice_in_dim(item_codes, group, width, 1)
        onehot = (codes_now[:, :, None] == code_range).astype(jnp.bfloat16)
        total = total + jnp.einsum(
            "rmk,imk->ri",
            tables[:, group : group + width],
            onehot,
            preferred_element_type=jnp.float32,
        )
    return total


def on_device(
    user_emb,
    codebooks,
    item_codes,
    item_place,
    candidates,
    item_features,
    cross_weights,
    cross_bias,
    out_weight,
):
    requests = user_emb.shape[0]
    local_sub = codebooks.shape[0]
    sub_width = codebooks.shape[2]
    parts = user_emb.reshape(requests, M, sub_width)
    empty = jnp.zeros((requests, item_codes.shape[0]), jnp.float32)
    first_sub = lax.axis_index("item") * local_sub
    mine = lax.dynamic_slice_in_dim(parts, first_sub, local_sub, 1)
    tables = jnp.einsum("rms,mks->rmk", mine, codebooks, preferred_element_type=jnp.float32).astype(
        jnp.bfloat16
    )
    scores = score_tables(empty, lax.all_gather(tables, "item", axis=1, tiled=True), item_codes)
    cand_dev = candidates.shape[1]
    rows_dev = item_features.shape[0]
    item_count = lax.axis_size("item")
    req_count = lax.axis_size("req")
    owners = item_count * req_count
    total_rows = requests * cand_dev
    capacity = 3 * total_rows // owners
    slots = jnp.take(item_place, candidates.reshape(-1), axis=0)
    owner = slots // rows_dev
    within = slots % rows_dev
    owner_hits = (owner[:, None] == jnp.arange(owners, dtype=jnp.int32)[None, :]).astype(jnp.int32)
    ranks = jnp.sum((jnp.cumsum(owner_hits, axis=0) - owner_hits) * owner_hits, axis=1)
    wanted = jnp.zeros((owners, capacity), jnp.int32).at[owner, ranks].set(within)
    found = jnp.take(
        item_features,
        lax.all_to_all(wanted, ("item", "req"), split_axis=0, concat_axis=0, tiled=True),
        axis=0,
    )
    fetched = lax.all_to_all(found, ("item", "req"), split_axis=0, concat_axis=0, tiled=True)
    item_rows = fetched[owner, ranks]
    repeated = jnp.repeat(user_emb, cand_dev, axis=0)
    first = jnp.concatenate([repeated, item_rows], axis=1)
    state = first.astype(jnp.float32)
    for layer in range(cross_weights.shape[0]):
        product = (
            jnp.dot(
                state.astype(jnp.bfloat16), cross_weights[layer], preferred_element_type=jnp.float32
            )
            + cross_bias[layer]
        )
        state = first * product + state
    logits = jnp.sum(state * out_weight, axis=1).reshape(requests, cand_dev)
    return (scores, logits)


def solution(mesh):
    placed = (
        P("req", None),
        P("item", None, None),
        P("item", None),
        P(),
        P("req", "item"),
        P(("item", "req"), None),
        P(),
        P(),
        P(),
    )
    return jax.shard_map(
        on_device,
        mesh=mesh,
        in_specs=placed,
        out_specs=(P("req", "item"), P("req", "item")),
        check_vma=False,
    )
```

profile of v0, /device:TPU:1, one launch (start us, length us, event | category | flops | bytes accessed | tf_op | source)
XLA Modules:
  0.0 162.4 jit_solution(7211599996360040882)
XLA Ops:
  0.6 0.0 copy-start
  0.6 0.9 copy.22
  1.5 0.1 reshape.233
  1.6 0.1 reshape.235
  1.7 0.1 reshape.234
  1.8 6.5 %gather_fusion = s32[512]{0:T(512)S(1)} fusion(s32[131072]{0:T(1024)} %param.12, s32[1024]{0:T(1024)S(1)} %pad_clamp_fusion.1), kind=kCustom, calls=%fused_computation | custom fusion | bytes 6144 | tf_op jit(solution)/shard_map/jit(_take)/gather | solution.py:55
  8.3 0.1 copy.25
  8.5 0.2 fusion.62
  8.8 0.2 fusion.61
  9.1 0.0 copy-start.2
  9.1 0.0 copy-start.1
  9.1 0.0 copy-start.4
  9.1 24.6 %scatter_fusion = s32[128,12]{0,1:T(8,128)S(1)} fusion(s32[128,12]{0,1:T(8,128)S(1)} %broadcast_in_dim.27, s32[512]{0:T(512)S(1)} %bitcast.106, s32[512]{0:T(512)S(1)} %get-tuple-element.20), kind=kCustom, calls=%fused_computation.3 | custom fusion | bytes 10240 | tf_op jit(solution)/shard_map/scatter | solution.py:60
  33.7 0.7 copy.27
  34.5 11.5 %all-to-all-start = ((s32[128,1,12]{2,1,0:T(1,128)}), s32[128,1,12]{2,1,0:T(1,128)S(1)}, u32[]{:S(2)}, u32[]{:S(2)}) async-start(s32[128,1,12]{2,1,0:T(1,128)} %copy.27), calls=%async_computation | async-start | bytes 131072 | tf_op jit(solution)/shard_map/all_to_all | solution.py:63
  46.0 0.0 copy-done.2
  46.0 0.1 copy.21
  46.1 0.1 fusion.74
  46.2 0.2 fusion.55
  46.4 25.8 %all_gather.3 = bf16[32,32,256]{2,0,1:T(8,128)(2,1)S(1)} all-gather(bf16[32,1,256]{2,0,1:T(8,128)(2,1)S(1)} %fusion.55), channel_id=1, replica_groups=mesh['item'=32,'req'=4] {'item'}, dimensions={1}, use_global_device_ids=true | all-gather | bytes 540672 | tf_op jit(solution)/shard_map/all_gather | solution.py:47
  72.2 0.0 all-to-all-done
  72.2 0.1 reshape.248
  72.3 5.7 %gather_fusion.1 = bf16[1536,768]{1,0:T(8,128)(2,1)} fusion(bf16[1024,768]{1,0:T(8,128)(2,1)S(1)} %copy-done, s32[2048]{0:T(1024)S(1)} %pad_clamp_fusion), kind=kCustom, calls=%fused_computation.1 | custom fusion | bytes 4724736 | tf_op jit(solution)/shard_map/jit(_take)/gather | solution.py:61
  78.0 4.9 %reshape.247 = bf16[128,12,768]{2,1,0:T(8,128)(2,1)} reshape(bf16[1536,768]{1,0:T(8,128)(2,1)} %gather_fusion.1) | data formatting | bytes 4718592 | tf_op jit(solution)/shard_map/jit(_take)/gather | solution.py:61
  82.9 0.1 copy.28
  83.0 0.1 copy.29
  83.1 3.3 %broadcast_select_fusion = bf16[128,12,768]{2,1,0:T(8,128)(2,1)} fusion(bf16[128,12,768]{2,1,0:T(8,128)(2,1)} %reshape.247, pred[128,12]{1,0:T(8,128)(4,1)S(1)} %copy.29), kind=kLoop, calls=%fused_computation.48 | loop fusion | flops 1179648 | bytes 4720128 | tf_op jit(solution)/shard_map/jit(_take)/select_n | solution.py:61
  86.4 7.5 %all-to-all-start.1 = ((bf16[128,12,768]{2,1,0:T(8,128)(2,1)}), bf16[128,12,768]{2,1,0:T(8,128)(2,1)}, u32[]{:S(2)}, u32[]{:S(2)}) async-start(bf16[128,12,768]{2,1,0:T(8,128)(2,1)} %broadcast_select_fusion), calls=%async_computation.1 | async-start | bytes 6291456 | tf_op jit(solution)/shard_map/all_to_all | solution.py:66
  94.0 5.9 %fusion.16 = f32[32,4096]{1,0:T(8,128)S(1)} fusion(bf16[32,32,256]{2,0,1:T(8,128)(2,1)S(1)} %all_gather.3, s32[4096,4]{0,1:T(4,128)S(1)} %get-tuple-element.14), kind=kOutput, calls=%fused_computation.28 | convolution fusion | flops 272629760 | bytes 1114112 | tf_op jit(solution)/shard_map/rmk,imk->ri/dot_general | solution.py:17
  99.9 5.9 %fusion.17 = f32[32,4096]{1,0:T(8,128)S(1)} fusion(bf16[32,32,256]{2,0,1:T(8,128)(2,1)S(1)} %all_gather.3, s32[4096,4]{0,1:T(4,128)S(1)} %get-tuple-element.15), kind=kOutput, calls=%fused_computation.29 | convolution fusion | flops 272629760 | bytes 1114112 | tf_op jit(solution)/shard_map/rmk,imk->ri/dot_general | solution.py:17
  105.8 5.9 %fusion.18 = f32[32,4096]{1,0:T(8,128)S(1)} fusion(bf16[32,32,256]{2,0,1:T(8,128)(2,1)S(1)} %all_gather.3, s32[4096,4]{0,1:T(4,128)S(1)} %get-tuple-element.9), kind=kOutput, calls=%fused_computation.30 | convolution fusion | flops 272629760 | bytes 1114112 | tf_op jit(solution)/shard_map/rmk,imk->ri/dot_general | solution.py:17
  111.8 5.9 %fusion.19 = f32[32,4096]{1,0:T(8,128)S(1)} fusion(bf16[32,32,256]{2,0,1:T(8,128)(2,1)S(1)} %all_gather.3, s32[4096,4]{0,1:T(4,128)S(1)} %get-tuple-element.10), kind=kOutput, calls=%fused_computation.31 | convolution fusion | flops 272629760 | bytes 1114112 | tf_op jit(solution)/shard_map/rmk,imk->ri/dot_general | solution.py:17
  117.7 5.9 %fusion.20 = f32[32,4096]{1,0:T(8,128)S(1)} fusion(bf16[32,32,256]{2,0,1:T(8,128)(2,1)S(1)} %all_gather.3, s32[4096,4]{0,1:T(4,128)S(1)} %get-tuple-element.11), kind=kOutput, calls=%fused_computation.32 | convolution fusion | flops 272629760 | bytes 1114112 | tf_op jit(solution)/shard_map/rmk,imk->ri/dot_general | solution.py:17
  123.7 5.9 %fusion.21 = f32[32,4096]{1,0:T(8,128)S(1)} fusion(bf16[32,32,256]{2,0,1:T(8,128)(2,1)S(1)} %all_gather.3, s32[4096,4]{0,1:T(4,128)S(1)} %get-tuple-element.12), kind=kOutput, calls=%fused_computation.33 | convolution fusion | flops 272629760 | bytes 1114112 | tf_op jit(solution)/shard_map/rmk,imk->ri/dot_general | solution.py:17
  129.6 5.9 %fusion.22 = f32[32,4096]{1,0:T(8,128)S(1)} fusion(bf16[32,32,256]{2,0,1:T(8,128)(2,1)S(1)} %all_gather.3, s32[4096,4]{0,1:T(4,128)S(1)} %get-tuple-element.13), kind=kOutput, calls=%fused_computation.34 | convolution fusion | flops 272629760 | bytes 1114112 | tf_op jit(solution)/shard_map/rmk,imk->ri/dot_general | solution.py:17
  135.6 5.5 %fusion.30 = f32[32,4096]{1,0:T(8,128)} fusion(f32[32,4096]{1,0:T(8,128)S(1)} %fusion.16, f32[32,4096]{1,0:T(8,128)S(1)} %fusion.17, f32[32,4096]{1,0:T(8,128)S(1)} %fusion.18, f32[32,4096]{1,0:T(8,128)S(1)} %fusion.19, f32[32,4096]{1,0:T(8,128)S(1)} %fusion.20, f32[32,4096]{1,0:T(8,128)S(1)} %fusion.21, f32[32,4096]{1,0:T(8,128)S(1)} %fusion.22, ...), kind=kOutput, calls=%fused_computation.42 | convolution fusion | flops 273547264 | bytes 4784128 | tf_op jit(solution)/shard_map/rmk,imk->ri/dot_general | solution.py:17
  141.0 0.0 all-to-all-done.1
  141.0 4.1 %copy.30 = bf16[128,12,768]{2,0,1:T(8,128)(2,1)} copy(bf16[128,12,768]{2,1,0:T(8,128)(2,1)} %all-to-all-done.1) | data formatting | bytes 4718592 | tf_op jit(solution)/shard_map/all_to_all | solution.py:66
  145.1 7.3 %gather_fusion.2 = bf16[512,768]{1,0:T(8,128)(2,1)S(1)} fusion(bf16[128,12,768]{2,0,1:T(8,128)(2,1)} %copy.30, s32[512]{0:T(512)S(1)} %bitcast.105), kind=kCustom, calls=%fused_computation.2 | custom fusion | bytes 1576960 | tf_op jit(solution)/shard_map/gather | solution.py:67
  152.4 0.0 slice-start
  152.4 3.0 %fusion.42 = f32[512,1024]{1,0:T(8,128)S(1)} fusion(bf16[4,1024,1024]{2,1,0:T(8,128)(2,1)} %param.15, bf16[512,768]{1,0:T(8,128)(2,1)S(1)} %gather_fusion.2, bf16[512,256]{1,0:T(8,128)(2,1)S(1)} %bitcast.110), kind=kOutput, calls=%fused_computation.60 | convolution fusion | flops 1075838976 | bytes 5242880 | tf_op jit(solution)/shard_map/dot_general | solution.py:73
  155.5 0.0 slice-start.1
  155.5 3.2 %fusion.31 = f32[512,1024]{1,0:T(8,128)S(1)} fusion(f32[512,1024]{1,0:T(8,128)S(1)} %fusion.42, bf16[4,1024,1024]{2,1,0:T(8,128)(2,1)} %param.15, f32[1024]{0:T(1024)S(1)} %bitcast.121, f32[1024]{0:T(1024)S(1)} %bitcast.122, bf16[512,768]{1,0:T(8,128)(2,1)S(1)} %gather_fusion.2, bf16[512,256]{1,0:T(8,128)(2,1)S(1)} %bitcast.111), kind=kOutput, calls=%fused_computation.49 | convolution fusion | flops 1083179008 | bytes 10498048 | tf_op jit(solution)/shard_map/dot_general | solution.py:73
  158.8 0.0 copy-start.5
  158.8 1.3 fusion.32
  160.1 1.5 fusion.35
  161.7 0.1 reshape.237
  161.8 0.7 copy.31
  (26 shorter events, 0.2 us)
Async XLA Ops:
  0.6 71.7 %copy-start = (bf16[1024,768]{1,0:T(8,128)(2,1)S(1)}, bf16[1024,768]{1,0:T(8,128)(2,1)}, u32[]{:S(2)}) copy-start(bf16[1024,768]{1,0:T(8,128)(2,1)} %param.14) | copy-start | bytes 4718596
  9.1 36.9 %copy-start.2 = (bf16[32,256]{1,0:T(8,128)(2,1)S(1)}, bf16[32,256]{1,0:T(8,128)(2,1)}, u32[]{:S(2)}) copy-start(bf16[32,256]{1,0:T(8,128)(2,1)} %param.9) | copy-start | bytes 49156
  9.1 37.0 %copy-start.1 = (s32[4096,32]{0,1:T(8,128)S(1)}, s32[4096,32]{0,1:T(8,128)}, u32[]{:S(2)}) copy-start(s32[4096,32]{0,1:T(8,128)} %param.11) | copy-start | bytes 1572868
  9.1 37.1 %copy-start.4 = (bf16[1,256,8]{1,2,0:T(8,128)(2,1)S(1)}, bf16[1,256,8]{1,2,0:T(8,128)(2,1)}, u32[]{:S(2)}) copy-start(bf16[1,256,8]{1,2,0:T(8,128)(2,1)} %param.10) | copy-start | bytes 12292
  34.5 37.7 %all-to-all-start = ((s32[128,1,12]{2,1,0:T(1,128)}), s32[128,1,12]{2,1,0:T(1,128)S(1)}, u32[]{:S(2)}, u32[]{:S(2)}) async-start(s32[128,1,12]{2,1,0:T(1,128)} %copy.27), calls=%async_computation | async-start | bytes 131072 | tf_op jit(solution)/shard_map/all_to_all | solution.py:63
  86.4 7.5 %copy-start.3 = (f32[4,1024]{1,0:T(4,128)S(1)}, f32[4,1024]{1,0:T(4,128)}, u32[]{:S(2)}) copy-start(f32[4,1024]{1,0:T(4,128)} %param.16) | copy-start | bytes 49156
  86.4 54.6 %all-to-all-start.1 = ((bf16[128,12,768]{2,1,0:T(8,128)(2,1)}), bf16[128,12,768]{2,1,0:T(8,128)(2,1)}, u32[]{:S(2)}, u32[]{:S(2)}) async-start(bf16[128,12,768]{2,1,0:T(8,128)(2,1)} %broadcast_select_fusion), calls=%async_computation.1 | async-start | bytes 6291456 | tf_op jit(solution)/shard_map/all_to_all | solution.py:66
  152.4 6.3 %slice-start = ((s8[8388608]{0:T(1024)(128)(4,1)}), s8[4194304]{0:T(1024)(128)(4,1)S(1)}, s32[]{:S(2)}) async-start(s8[8388608]{0:T(1024)(128)(4,1)} %bitcast.123), calls=%async_computation.2 | async-start | bytes 8388608
  155.5 3.3 %slice-start.1 = ((s8[8388608]{0:T(1024)(128)(4,1)}), s8[4194304]{0:T(1024)(128)(4,1)S(1)}, s32[]{:S(2)}) async-start(s8[8388608]{0:T(1024)(128)(4,1)} %bitcast.123), calls=%async_computation.3 | async-start | bytes 8388608
  158.8 1.4 copy-start.5
where the time goes:
time: 163 us; the launch traced here: 162 us
  local copies, waits for them, and re-layouts  56.4 us (35%)
  matrix products  56.4 us (35%)
  blocking collectives  25.8 us (16%)
  starting transfers between devices  19 us (12%)
  other arithmetic  3.91 us (2%)
    dot_general x8, matrix products, score_tables(): jnp.einsum('rmk,imk->ri', tables[:, group:group + width], onehot, preferr...  47 us
    all_gather x1, blocking collectives, on_device(): lax.all_gather(tables, 'item', axis=1, tiled=True)  25.8 us
    scatter x1, local copies, waits for them, and re-layouts, on_device(): jnp.zeros((owners, capacity), jnp.int32).at[owner, ranks].set(within)  24.6 us
    all_to_all x1, starting transfers between devices, on_device(): lax.all_to_all(wanted, ('item', 'req'), split_axis=0, concat_axis=0, tile...  11.5 us
    gather x2, local copies, waits for them, and re-layouts, on_device(): jnp.take(item_features, lax.all_to_all(wanted, ('item', 'req'), split_axi...  10.5 us
    dot_general x4, matrix products, on_device(): jnp.dot(state.astype(jnp.bfloat16), cross_weights[layer], preferred_eleme...  9.15 us
    all_to_all x1, starting transfers between devices, on_device(): lax.all_to_all(found, ('item', 'req'), split_axis=0, concat_axis=0, tiled...  7.49 us
    gather x1, local copies, waits for them, and re-layouts, on_device(): item_rows = fetched[owner, ranks]  7.29 us
  transfers between devices with their start and end apart: 2, of which 0 were waited for; matrix products, arithmetic and copies ran while one was open for 29% of the time, Pallas kernels for 0%

commit v1 on v0

--- a/solution.py
+++ b/solution.py
@@ -4,6 +4,13 @@
 from jax.sharding import PartitionSpec as P
 
 M = 32
+
+
+def all_by_exchange(shard, axis, dim):
+    n_dev = lax.axis_size(axis)
+    shards = jnp.stack([shard for _ in range(n_dev)])
+    shards = lax.all_to_all(shards, axis, split_axis=0, concat_axis=0)
+    return jnp.concatenate(shards, axis=dim)
 
 
 def score_tables(total, tables, item_codes):
@@ -44,7 +51,7 @@
     tables = jnp.einsum("rms,mks->rmk", mine, codebooks, preferred_element_type=jnp.float32).astype(
         jnp.bfloat16
     )
-    scores = score_tables(empty, lax.all_gather(tables, "item", axis=1, tiled=True), item_codes)
+    scores = score_tables(empty, all_by_exchange(tables, "item", 1), item_codes)
     cand_dev = candidates.shape[1]
     rows_dev = item_features.shape[0]
     item_count = lax.axis_size("item")

time: 163 us -> 152 us (0.933)
  blocking collectives: 25.8 us -> 0 us
  waiting for transfers between devices: 0.01 us -> 9.13 us
  starting transfers between devices: 19 us -> 23.9 us
    all_gather x1 -> x0, blocking collectives: 25.8 us -> none  [on_device(): lax.all_gather(tables, 'item', axis=1, tiled=True)]
    all_to_all x1, waiting for transfers between devices: 0.01 us -> 9.12 us  [on_device(): lax.all_to_all(wanted, ('item', 'req'), split_axis=0, concat_axis=0, tile...]
    all_to_all x0 -> x1, starting transfers between devices: none -> 4.28 us  [all_by_exchange(): shards = lax.all_to_all(shards, axis, split_axis=0, concat_axis=0)]
  transfers between devices with their start and end apart: 2 -> 3, of which waited for: 0 -> 1; matrix products, arithmetic and copies ran while one was open for 29% -> 41% of each run, Pallas kernels for 0% -> 0%
where the time goes in v1:
time: 152 us
  local copies, waits for them, and re-layouts  57.2 us (38%)
  matrix products  56.4 us (37%)
  starting transfers between devices  23.9 us (16%)
  waiting for transfers between devices  9.13 us (6%)
  other arithmetic  3.92 us (3%)
    dot_general x8, matrix products, score_tables(): jnp.einsum('rmk,imk->ri', tables[:, group:group + width], onehot, preferr...  47 us
    scatter x1, local copies, waits for them, and re-layouts, on_device(): jnp.zeros((owners, capacity), jnp.int32).at[owner, ranks].set(within)  24.6 us
    all_to_all x1, starting transfers between devices, on_device(): lax.all_to_all(wanted, ('item', 'req'), split_axis=0, concat_axis=0, tile...  11.5 us
    gather x2, local copies, waits for them, and re-layouts, on_device(): jnp.take(item_features, lax.all_to_all(wanted, ('item', 'req'), split_axi...  10.5 us
    dot_general x4, matrix products, on_device(): jnp.dot(state.astype(jnp.bfloat16), cross_weights[layer], preferred_eleme...  9.14 us
    all_to_all x1, waiting for transfers between devices, on_device(): lax.all_to_all(wanted, ('item', 'req'), split_axis=0, concat_axis=0, tile...  9.12 us
    all_to_all x1, starting transfers between devices, on_device(): lax.all_to_all(found, ('item', 'req'), split_axis=0, concat_axis=0, tiled...  8.09 us
    gather x1, local copies, waits for them, and re-layouts, on_device(): item_rows = fetched[owner, ranks]  7.3 us
  transfers between devices with their start and end apart: 3, of which 1 were waited for; matrix products, arithmetic and copies ran while one was open for 41% of the time, Pallas kernels for 0%

profile of v1, /device:TPU:1, one launch (start us, length us, event | category | flops | bytes accessed | tf_op | source)
XLA Modules:
  0.0 151.5 jit_solution(1640663232162696519)
XLA Ops:
  0.6 0.0 copy-start
  0.6 0.9 copy.23
  1.5 0.1 reshape.244
  1.6 0.1 reshape.246
  1.7 0.1 reshape.245
  1.8 6.5 %gather_fusion = s32[512]{0:T(512)S(1)} fusion(s32[131072]{0:T(1024)} %param.12, s32[1024]{0:T(1024)S(1)} %pad_clamp_fusion.1), kind=kCustom, calls=%fused_computation | custom fusion | bytes 6144 | tf_op jit(solution)/shard_map/jit(_take)/gather | solution.py:62
  8.3 0.1 copy.26
  8.5 0.2 fusion.69
  8.8 0.2 fusion.68
  9.1 0.0 copy-start.2
  9.1 0.0 copy-start.1
  9.1 0.0 copy-start.4
  9.1 24.6 %scatter_fusion = s32[128,12]{0,1:T(8,128)S(1)} fusion(s32[128,12]{0,1:T(8,128)S(1)} %broadcast_in_dim.27, s32[512]{0:T(512)S(1)} %bitcast.113, s32[512]{0:T(512)S(1)} %get-tuple-element.20), kind=kCustom, calls=%fused_computation.3 | custom fusion | bytes 10240 | tf_op jit(solution)/shard_map/scatter | solution.py:67
  33.7 0.7 copy.28
  34.5 11.5 %all-to-all-start.1 = ((s32[128,1,12]{2,1,0:T(1,128)}), s32[128,1,12]{2,1,0:T(1,128)S(1)}, u32[]{:S(2)}, u32[]{:S(2)}) async-start(s32[128,1,12]{2,1,0:T(1,128)} %copy.28), calls=%async_computation.1 | async-start | bytes 131072 | tf_op jit(solution)/shard_map/all_to_all | solution.py:70
  46.0 0.1 copy.21
  46.1 0.1 fusion.81
  46.2 0.2 convolution_convert_fusion
  46.4 9.1 %all-to-all-done.1 = s32[128,1,12]{2,1,0:T(1,128)S(1)} async-done(((s32[128,1,12]{2,1,0:T(1,128)}), s32[128,1,12]{2,1,0:T(1,128)S(1)}, u32[]{:S(2)}, u32[]{:S(2)}) %all-to-all-start.1) | async-done | bytes 6176 | tf_op jit(solution)/shard_map/all_to_all | solution.py:70
  55.5 0.9 stack.2
  56.4 4.3 %all-to-all-start = ((bf16[32,32,1,256]{3,1,2,0:T(8,128)(2,1)}), bf16[32,32,1,256]{3,1,2,0:T(8,128)(2,1)S(1)}, u32[]{:S(2)}, u32[]{:S(2)}) async-start(bf16[32,32,1,256]{3,1,2,0:T(8,128)(2,1)} %stack.2), calls=%async_computation | async-start | bytes 1048576 | tf_op jit(solution)/shard_map/all_to_all | solution.py:12
  60.7 0.1 reshape.259
  60.8 5.7 %gather_fusion.1 = bf16[1536,768]{1,0:T(8,128)(2,1)} fusion(bf16[1024,768]{1,0:T(8,128)(2,1)S(1)} %copy-done, s32[2048]{0:T(1024)S(1)} %pad_clamp_fusion), kind=kCustom, calls=%fused_computation.1 | custom fusion | bytes 4724736 | tf_op jit(solution)/shard_map/jit(_take)/gather | solution.py:68
  66.5 4.9 %reshape.258 = bf16[128,12,768]{2,1,0:T(8,128)(2,1)} reshape(bf16[1536,768]{1,0:T(8,128)(2,1)} %gather_fusion.1) | data formatting | bytes 4718592 | tf_op jit(solution)/shard_map/jit(_take)/gather | solution.py:68
  71.4 0.1 copy.29
  71.4 0.1 copy.30
  71.6 3.3 %broadcast_select_fusion = bf16[128,12,768]{2,1,0:T(8,128)(2,1)} fusion(bf16[128,12,768]{2,1,0:T(8,128)(2,1)} %reshape.258, pred[128,12]{1,0:T(8,128)(4,1)S(1)} %copy.30), kind=kLoop, calls=%fused_computation.48 | loop fusion | flops 1179648 | bytes 4720128 | tf_op jit(solution)/shard_map/jit(_take)/select_n | solution.py:68
  74.9 0.0 all-to-all-done
  74.9 8.1 %all-to-all-start.2 = ((bf16[128,12,768]{2,1,0:T(8,128)(2,1)}), bf16[128,12,768]{2,1,0:T(8,128)(2,1)}, u32[]{:S(2)}, u32[]{:S(2)}) async-start(bf16[128,12,768]{2,1,0:T(8,128)(2,1)} %broadcast_select_fusion), calls=%async_computation.2 | async-start | bytes 6291456 | tf_op jit(solution)/shard_map/all_to_all | solution.py:73
  83.0 5.9 %fusion.17 = f32[32,4096]{1,0:T(8,128)S(1)} fusion(s32[4096,4]{0,1:T(4,128)S(1)} %get-tuple-element.15, bf16[32,32,1,256]{3,1,2,0:T(8,128)(2,1)S(1)} %all-to-all-done), kind=kOutput, calls=%fused_computation.29 | convolution fusion | flops 272629760 | bytes 1114112 | tf_op jit(solution)/shard_map/rmk,imk->ri/dot_general | solution.py:24
  89.0 5.9 %fusion.18 = f32[32,4096]{1,0:T(8,128)S(1)} fusion(s32[4096,4]{0,1:T(4,128)S(1)} %get-tuple-element.9, bf16[32,32,1,256]{3,1,2,0:T(8,128)(2,1)S(1)} %all-to-all-done), kind=kOutput, calls=%fused_computation.30 | convolution fusion | flops 272629760 | bytes 1114112 | tf_op jit(solution)/shard_map/rmk,imk->ri/dot_general | solution.py:24
  94.9 5.9 %fusion.19 = f32[32,4096]{1,0:T(8,128)S(1)} fusion(s32[4096,4]{0,1:T(4,128)S(1)} %get-tuple-element.10, bf16[32,32,1,256]{3,1,2,0:T(8,128)(2,1)S(1)} %all-to-all-done), kind=kOutput, calls=%fused_computation.31 | convolution fusion | flops 272629760 | bytes 1114112 | tf_op jit(solution)/shard_map/rmk,imk->ri/dot_general | solution.py:24
  100.9 5.9 %fusion.20 = f32[32,4096]{1,0:T(8,128)S(1)} fusion(s32[4096,4]{0,1:T(4,128)S(1)} %get-tuple-element.11, bf16[32,32,1,256]{3,1,2,0:T(8,128)(2,1)S(1)} %all-to-all-done), kind=kOutput, calls=%fused_computation.32 | convolution fusion | flops 272629760 | bytes 1114112 | tf_op jit(solution)/shard_map/rmk,imk->ri/dot_general | solution.py:24
  106.8 5.9 %fusion.21 = f32[32,4096]{1,0:T(8,128)S(1)} fusion(s32[4096,4]{0,1:T(4,128)S(1)} %get-tuple-element.12, bf16[32,32,1,256]{3,1,2,0:T(8,128)(2,1)S(1)} %all-to-all-done), kind=kOutput, calls=%fused_computation.33 | convolution fusion | flops 272629760 | bytes 1114112 | tf_op jit(solution)/shard_map/rmk,imk->ri/dot_general | solution.py:24
  112.8 5.9 %fusion.22 = f32[32,4096]{1,0:T(8,128)S(1)} fusion(s32[4096,4]{0,1:T(4,128)S(1)} %get-tuple-element.13, bf16[32,32,1,256]{3,1,2,0:T(8,128)(2,1)S(1)} %all-to-all-done), kind=kOutput, calls=%fused_computation.34 | convolution fusion | flops 272629760 | bytes 1114112 | tf_op jit(solution)/shard_map/rmk,imk->ri/dot_general | solution.py:24
  118.7 5.9 %fusion.16 = f32[32,4096]{1,0:T(8,128)S(1)} fusion(s32[4096,4]{0,1:T(4,128)S(1)} %get-tuple-element.14, bf16[32,32,1,256]{3,1,2,0:T(8,128)(2,1)S(1)} %all-to-all-done), kind=kOutput, calls=%fused_computation.28 | convolution fusion | flops 272629760 | bytes 1114112 | tf_op jit(solution)/shard_map/rmk,imk->ri/dot_general | solution.py:24
  124.7 5.5 %fusion.30 = f32[32,4096]{1,0:T(8,128)} fusion(f32[32,4096]{1,0:T(8,128)S(1)} %fusion.16, f32[32,4096]{1,0:T(8,128)S(1)} %fusion.17, f32[32,4096]{1,0:T(8,128)S(1)} %fusion.18, f32[32,4096]{1,0:T(8,128)S(1)} %fusion.19, f32[32,4096]{1,0:T(8,128)S(1)} %fusion.20, f32[32,4096]{1,0:T(8,128)S(1)} %fusion.21, f32[32,4096]{1,0:T(8,128)S(1)} %fusion.22, ...), kind=kOutput, calls=%fused_computation.42 | convolution fusion | flops 273547264 | bytes 4784128 | tf_op jit(solution)/shard_map/rmk,imk->ri/dot_general | solution.py:24
  130.1 4.1 %copy.31 = bf16[128,12,768]{2,0,1:T(8,128)(2,1)} copy(bf16[128,12,768]{2,1,0:T(8,128)(2,1)} %all-to-all-done.2) | data formatting | bytes 4718592 | tf_op jit(solution)/shard_map/all_to_all | solution.py:73
  134.2 7.3 %gather_fusion.2 = bf16[512,768]{1,0:T(8,128)(2,1)S(1)} fusion(bf16[128,12,768]{2,0,1:T(8,128)(2,1)} %copy.31, s32[512]{0:T(512)S(1)} %bitcast.112), kind=kCustom, calls=%fused_computation.2 | custom fusion | bytes 1576960 | tf_op jit(solution)/shard_map/gather | solution.py:74
  141.5 0.0 slice-start
  141.6 3.0 %fusion.42 = f32[512,1024]{1,0:T(8,128)S(1)} fusion(bf16[4,1024,1024]{2,1,0:T(8,128)(2,1)} %param.15, bf16[512,768]{1,0:T(8,128)(2,1)S(1)} %gather_fusion.2, bf16[512,256]{1,0:T(8,128)(2,1)S(1)} %bitcast.117), kind=kOutput, calls=%fused_computation.60 | convolution fusion | flops 1075838976 | bytes 5242880 | tf_op jit(solution)/shard_map/dot_general | solution.py:80
  144.6 0.0 slice-start.1
  144.6 3.2 %fusion.31 = f32[512,1024]{1,0:T(8,128)S(1)} fusion(f32[512,1024]{1,0:T(8,128)S(1)} %fusion.42, bf16[4,1024,1024]{2,1,0:T(8,128)(2,1)} %param.15, f32[1024]{0:T(1024)S(1)} %bitcast.128, f32[1024]{0:T(1024)S(1)} %bitcast.129, bf16[512,768]{1,0:T(8,128)(2,1)S(1)} %gather_fusion.2, bf16[512,256]{1,0:T(8,128)(2,1)S(1)} %bitcast.118), kind=kOutput, calls=%fused_computation.49 | convolution fusion | flops 1083179008 | bytes 10498048 | tf_op jit(solution)/shard_map/dot_general | solution.py:80
  147.9 0.0 copy-start.5
  147.9 1.3 fusion.32
  149.2 1.5 %fusion.35 = f32[512]{0:T(512)S(1)} fusion(f32[512,1024]{1,0:T(8,128)S(1)} %fusion.32, bf16[4,1024,1024]{2,1,0:T(8,128)(2,1)S(1)} %bitcast.131, f32[1024]{0:T(1024)S(1)} %copy-done.5, f32[1024]{0:T(1024)S(1)} %bitcast.126, bf16[512,768]{1,0:T(8,128)(2,1)S(1)} %gather_fusion.2, bf16[512,256]{1,0:T(8,128)(2,1)S(1)} %bitcast.120), kind=kOutput, calls=%fused_computation.53 | convolution fusion | flops 1078984192 | bytes 7350272 | tf_op jit(solution)/shard_map/dot_general | solution.py:80
  150.8 0.1 reshape.248
  150.9 0.7 copy.32
  (28 shorter events, 0.3 us)
Async XLA Ops:
  0.6 60.2 %copy-start = (bf16[1024,768]{1,0:T(8,128)(2,1)S(1)}, bf16[1024,768]{1,0:T(8,128)(2,1)}, u32[]{:S(2)}) copy-start(bf16[1024,768]{1,0:T(8,128)(2,1)} %param.14) | copy-start | bytes 4718596
  9.1 36.9 %copy-start.2 = (bf16[32,256]{1,0:T(8,128)(2,1)S(1)}, bf16[32,256]{1,0:T(8,128)(2,1)}, u32[]{:S(2)}) copy-start(bf16[32,256]{1,0:T(8,128)(2,1)} %param.9) | copy-start | bytes 49156
  9.1 37.0 %copy-start.1 = (s32[4096,32]{0,1:T(8,128)S(1)}, s32[4096,32]{0,1:T(8,128)}, u32[]{:S(2)}) copy-start(s32[4096,32]{0,1:T(8,128)} %param.11) | copy-start | bytes 1572868
  9.1 37.1 %copy-start.4 = (bf16[1,256,8]{1,2,0:T(8,128)(2,1)S(1)}, bf16[1,256,8]{1,2,0:T(8,128)(2,1)}, u32[]{:S(2)}) copy-start(bf16[1,256,8]{1,2,0:T(8,128)(2,1)} %param.10) | copy-start | bytes 12292
  34.5 21.1 %all-to-all-start.1 = ((s32[128,1,12]{2,1,0:T(1,128)}), s32[128,1,12]{2,1,0:T(1,128)S(1)}, u32[]{:S(2)}, u32[]{:S(2)}) async-start(s32[128,1,12]{2,1,0:T(1,128)} %copy.28), calls=%async_computation.1 | async-start | bytes 131072 | tf_op jit(solution)/shard_map/all_to_all | solution.py:70
  56.4 18.5 %all-to-all-start = ((bf16[32,32,1,256]{3,1,2,0:T(8,128)(2,1)}), bf16[32,32,1,256]{3,1,2,0:T(8,128)(2,1)S(1)}, u32[]{:S(2)}, u32[]{:S(2)}) async-start(bf16[32,32,1,256]{3,1,2,0:T(8,128)(2,1)} %stack.2), calls=%async_computation | async-start | bytes 1048576 | tf_op jit(solution)/shard_map/all_to_all | solution.py:12
  74.9 8.1 %copy-start.3 = (f32[4,1024]{1,0:T(4,128)S(1)}, f32[4,1024]{1,0:T(4,128)}, u32[]{:S(2)}) copy-start(f32[4,1024]{1,0:T(4,128)} %param.16) | copy-start | bytes 49156
  74.9 55.2 %all-to-all-start.2 = ((bf16[128,12,768]{2,1,0:T(8,128)(2,1)}), bf16[128,12,768]{2,1,0:T(8,128)(2,1)}, u32[]{:S(2)}, u32[]{:S(2)}) async-start(bf16[128,12,768]{2,1,0:T(8,128)(2,1)} %broadcast_select_fusion), calls=%async_computation.2 | async-start | bytes 6291456 | tf_op jit(solution)/shard_map/all_to_all | solution.py:73
  141.5 6.3 %slice-start = ((s8[8388608]{0:T(1024)(128)(4,1)}), s8[4194304]{0:T(1024)(128)(4,1)S(1)}, s32[]{:S(2)}) async-start(s8[8388608]{0:T(1024)(128)(4,1)} %bitcast.130), calls=%async_computation.3 | async-start | bytes 8388608
  144.6 3.3 %slice-start.1 = ((s8[8388608]{0:T(1024)(128)(4,1)}), s8[4194304]{0:T(1024)(128)(4,1)S(1)}, s32[]{:S(2)}) async-start(s8[8388608]{0:T(1024)(128)(4,1)} %bitcast.130), calls=%async_computation.4 | async-start | bytes 8388608
  147.9 1.4 copy-start.5
